TPU v7x, 256 devices: a whole 4x4x8 slice. The times are simulated.
256 devices in a mesh: fsdp: 16 (over x_lo, z), rep: 16 (over y, x_hi, core).
Axes of the slice: x: 4 (x_hi: 2, x_lo: 2; x = x_hi * 2 + x_lo), y: 4, z: 8, core: 2. Of those that a mesh axis runs over, the one named last changes fastest.
Arguments:
- samples: bfloat16 [6144, 4096], P(('fsdp', 'rep')), may hold values from -10 to 10
- dual_weight: bfloat16 [8192, 4096], P('fsdp'), may hold values from -0.09375 to 0.09375
- dual_vector: float32 [2, 8192], P(None, 'fsdp'), may hold values from 0 to 2
- map_weight: float32 [8192, 4096], P(('fsdp', 'rep')), may hold values from -0.09375 to 0.09375
- map_vector: float32 [2, 8192], P(None, ('fsdp', 'rep')), may hold values from 0.001 to 2
- moment_weight: float32 [8192, 4096], P(('fsdp', 'rep')), may hold values from -0.006 to 0.006
- square_weight: float32 [8192, 4096], P(('fsdp', 'rep')), may hold values from 0.0001 to 0.01
- moment_vector: float32 [2, 8192], P(None, ('fsdp', 'rep')), may hold values from -0.03 to 0.03
- square_vector: float32 [2, 8192], P(None, ('fsdp', 'rep')), may hold values from 0.0001 to 0.01
Outputs:
- next_weight: float32 [8192, 4096], P(('fsdp', 'rep'))
- next_vector: float32 [2, 8192], P(None, ('fsdp', 'rep'))
- next_moment_weight: float32 [8192, 4096], P(('fsdp', 'rep'))
- next_square_weight: float32 [8192, 4096], P(('fsdp', 'rep'))
- next_moment_vector: float32 [2, 8192], P(None, ('fsdp', 'rep'))
- next_square_vector: float32 [2, 8192], P(None, ('fsdp', 'rep'))
All inputs are finite; a program needn't handle non-finite values.
Results may differ from a plain program's by a relative error of at most 0.004.
Values may be sent and summed in bfloat16 or wider, within the bound.
No kernel may reach another device: no remote copies, remote signals or barrier semaphores. Data moves between devices by JAX's collectives and lax.ppermute only.
A program may use at most 64 MiB of HBM per device.

v0:
```python
import jax
import jax.numpy as jnp
from jax import lax
from jax.sharding import PartitionSpec as P

beta_one = 0.9
beta_two = 0.999
learn_rate = 0.001
epsilon = 1e-08
adam_step = 10


def contract_last(left, right):
    return lax.dot_general(
        left, right, (((1,), (1,)), ((), ())), preferred_element_type=jnp.float32
    )


def contract_first(left, right):
    return lax.dot_general(
        left, right, (((0,), (0,)), ((), ())), preferred_element_type=jnp.float32
    )


def adam_update(param, grad, moment, square):
    moment_new = beta_one * moment + (1.0 - beta_one) * grad
    square_new = beta_two * square + (1.0 - beta_two) * grad * grad
    fix_one = 1.0 - beta_one**adam_step
    fix_two = 1.0 - beta_two**adam_step
    update = learn_rate * (moment_new / fix_one) / (jnp.sqrt(square_new / fix_two) + epsilon)
    return (param - update, moment_new, square_new)


def body(
    samples,
    dual_weight,
    dual_vector,
    map_weight,
    map_vector,
    moment_weight,
    square_weight,
    moment_vector,
    square_vector,
):
    group_rows = lax.all_gather(samples, "fsdp", axis=0, tiled=True)
    weight_slab, vector_slab = (
        lax.all_gather(map_weight.astype(jnp.bfloat16), "rep", axis=0, tiled=True),
        lax.all_gather(map_vector.astype(jnp.bfloat16), "rep", axis=1, tiled=True),
    )
    readout = vector_slab[0].astype(jnp.float32)
    offset = vector_slab[1].astype(jnp.float32)
    inverse_rows = 1.0 / (group_rows.shape[0] * lax.axis_size("rep"))
    hidden = contract_last(group_rows, weight_slab) + offset
    sigma = jax.nn.sigmoid(hidden)
    scaled = (readout * sigma).astype(jnp.bfloat16)
    group_float = group_rows.astype(jnp.float32)
    mapped = group_float + lax.psum(
        jnp.dot(scaled, weight_slab, preferred_element_type=jnp.float32).astype(jnp.bfloat16),
        "fsdp",
    ).astype(jnp.float32)
    mapped_low = mapped.astype(jnp.bfloat16)
    dual_hidden = contract_last(mapped_low, dual_weight) + dual_vector[1]
    dual_scaled = (dual_vector[0] * jax.nn.sigmoid(dual_hidden)).astype(jnp.bfloat16)
    dual_grad = mapped + lax.psum(
        jnp.dot(dual_scaled, dual_weight, preferred_element_type=jnp.float32).astype(jnp.bfloat16),
        "fsdp",
    ).astype(jnp.float32)
    residual = (group_float - dual_grad).astype(jnp.bfloat16)
    pulled = contract_last(residual, weight_slab)
    slope = sigma * (1.0 - sigma)
    curve_float = readout * slope * pulled
    curve_term = curve_float.astype(jnp.bfloat16)
    left_stack = jnp.concatenate([scaled, curve_term], axis=0)
    right_stack = jnp.concatenate([residual, group_rows], axis=0)
    grad_slab = contract_first(left_stack, right_stack) * inverse_rows
    grad_small = (
        jnp.stack([jnp.sum(sigma * pulled, axis=0), jnp.sum(curve_float, axis=0)]) * inverse_rows
    )
    owner_weight, owner_vector = (
        lax.psum_scatter(grad_slab, "rep", scatter_dimension=0, tiled=True),
        lax.psum_scatter(grad_small, "rep", scatter_dimension=1, tiled=True),
    )
    next_weight, next_moment_weight, next_square_weight = adam_update(
        map_weight, owner_weight, moment_weight, square_weight
    )
    raw_vector, next_moment_vector, next_square_vector = adam_update(
        map_vector, owner_vector, moment_vector, square_vector
    )
    next_vector = jnp.concatenate([jnp.maximum(raw_vector[0:1], 0.0), raw_vector[1:2]], axis=0)
    return (
        next_weight,
        next_vector,
        next_moment_weight,
        next_square_weight,
        next_moment_vector,
        next_square_vector,
    )


def solution(mesh):
    return jax.shard_map(
        body,
        mesh=mesh,
        in_specs=(
            P(("fsdp", "rep"), None),
            P("fsdp", None),
            P(None, "fsdp"),
            P(("fsdp", "rep"), None),
            P(None, ("fsdp", "rep")),
            P(("fsdp", "rep"), None),
            P(("fsdp", "rep"), None),
            P(None, ("fsdp", "rep")),
            P(None, ("fsdp", "rep")),
        ),
        out_specs=(
            P(("fsdp", "rep"), None),
            P(None, ("fsdp", "rep")),
            P(("fsdp", "rep"), None),
            P(("fsdp", "rep"), None),
            P(None, ("fsdp", "rep")),
            P(None, ("fsdp", "rep")),
        ),
        check_vma=False,
    )
```

profile of v0, /device:TPU:2, one launch (start us, length us, event | category | flops | bytes accessed | tf_op | source)
XLA Modules:
  0.0 657.9 jit_solution(16748205175265367710)
XLA Ops:
  7.2 0.0 all-gather.4.cloned.1.call-start
  7.2 0.7 all-gather.4.cloned.1.call-update
  7.9 0.0 all-gather.6.cloned.1.call-start
  7.9 1.8 convert_element_type.41
  9.7 0.0 all-gather.6.cloned.1.call-update
  9.7 0.0 all-reduce.3.cloned.1.call-start
  9.8 0.7 convert_bitcast_fusion
  10.5 23.4 %all-gather = bf16[16,32,2]{1,2,0:T(2,128)(2,1)S(1)} all-gather(bf16[1,32,2]{1,2,0:T(2,128)(2,1)S(1)} %convert_bitcast_fusion), channel_id=1, replica_groups=mesh['fsdp'=16,'rep'=16] {'rep'}, dimensions={0}, use_global_device_ids=true | all-gather | bytes 2176 | tf_op jit(solution)/shard_map/all_gather | solution.py:48
  33.9 0.1 reshape.15
  34.0 52.4 %all-gather.4.cloned.1.call-done = bf16[384,4096]{1,0:T(8,128)(2,1)} async-done(((bf16[24,4096]{1,0:T(8,128)(2,1)}), bf16[384,4096]{1,0:T(8,128)(2,1)}) %all-gather.4.cloned.1.call-update) | async-done | bytes 3145744 | tf_op jit(solution)/shard_map/all_gather | solution.py:45
  86.5 61.3 %all-gather.6.cloned.1.call-done = bf16[512,4096]{1,0:T(8,128)(2,1)} async-done(((bf16[32,4096]{1,0:T(8,128)(2,1)}), bf16[512,4096]{1,0:T(8,128)(2,1)}) %all-gather.6.cloned.1.call-update) | async-done | bytes 4194320 | tf_op jit(solution)/shard_map/all_gather | solution.py:47
  147.8 0.0 copy-start.9
  147.8 6.1 multiply_convert_fusion
  153.9 0.0 copy-done.9
  153.9 0.0 copy-start.5
  153.9 0.0 copy-start
  153.9 3.6 convolution_convert_fusion.1
  157.5 0.0 all-reduce.3.cloned.1.call-update
  157.5 0.0 all-reduce.5.cloned.1.call-start
  157.5 0.0 copy-done.5
  157.6 144.9 %all-reduce.3.cloned.1.call-done = bf16[384,4096]{1,0:T(8,128)(2,1)} async-done(((bf16[384,4096]{1,0:T(8,128)(2,1)}), bf16[384,4096]{1,0:T(8,128)(2,1)}) %all-reduce.3.cloned.1.call-update) | async-done | bytes 3145744 | tf_op jit(solution)/shard_map/psum | solution.py:57
  302.5 0.0 copy-done
  302.5 9.7 %convolution_convert_fusion = bf16[384,4096]{1,0:T(8,128)(2,1)} fusion(bf16[512,4096]{1,0:T(8,128)(2,1)} %param.10, bf16[384,4096]{1,0:T(8,128)(2,1)} %all-reduce.3.cloned.1.call-done, bf16[384,4096]{1,0:T(8,128)(2,1)S(1)} %copy-done, f32[512]{0:T(512)S(1)} %bitcast.30, f32[512]{0:T(512)S(1)} %bitcast.29), kind=kOutput, calls=%fused_computation.8 | convolution fusion | flops 3230269440 | bytes 13635584 | tf_op jit(solution)/shard_map/dot_general | solution.py:65
  312.2 0.0 all-reduce.5.cloned.1.call-update
  312.2 0.0 reduce-scatter.7.cloned.1.call-start
  312.3 144.4 %all-reduce.5.cloned.1.call-done = bf16[384,4096]{1,0:T(8,128)(2,1)} async-done(((bf16[384,4096]{1,0:T(8,128)(2,1)}), bf16[384,4096]{1,0:T(8,128)(2,1)}) %all-reduce.5.cloned.1.call-update) | async-done | bytes 3145744 | tf_op jit(solution)/shard_map/psum | solution.py:64
  456.7 0.0 copy-start.10
  456.7 0.0 copy-start.11
  456.7 4.7 fusion
  461.4 0.0 copy-start.1
  461.4 0.0 copy-done.10
  461.5 0.0 copy-done.11
  461.5 2.6 multiply_reduce_fusion
  464.1 0.0 copy-done.1
  464.1 0.9 copy.17
  465.0 0.0 reduce-scatter.7.cloned.1.call-update
  465.0 0.2 reduce-scatter.5.cloned.1.call-start
  465.2 8.8 %convolution_multiply_fusion = f32[512,4096]{1,0:T(8,128)} fusion(bf16[384,4096]{1,0:T(8,128)(2,1)S(1)} %copy-done, bf16[384,4096]{1,0:T(8,128)(2,1)} %copy-done.1, bf16[384,512]{1,0:T(8,128)(2,1)} %get-tuple-element.14, bf16[384,512]{1,0:T(8,128)(2,1)S(1)} %get-tuple-element.21), kind=kOutput, calls=%fused_computation.2 | convolution fusion | flops 3237478400 | bytes 15466496 | tf_op jit(solution)/shard_map/dot_general | solution.py:20
  474.0 0.0 copy-start.6
  474.0 0.0 copy-start.7
  474.0 0.0 copy-start.8
  474.0 0.0 copy-start.2
  474.0 0.0 copy-start.3
  474.0 0.0 copy-start.4
  474.0 0.0 reduce-scatter.5.cloned.1.call-update
  474.0 61.3 %reduce-scatter.7.cloned.1.call-done = f32[32,2]{1,0:T(8,128)} async-done(((f32[512,2]{1,0:T(8,128)}), f32[32,2]{1,0:T(8,128)}) %reduce-scatter.7.cloned.1.call-update) | async-done | bytes 272
  535.4 0.8 copy.18
  536.2 0.0 copy-done.6
  536.2 0.0 copy-done.7
  536.2 0.0 copy-done.8
  536.2 0.6 divide_subtract_fusion.1
  536.8 0.6 pad_maximum_fusion
  537.3 111.4 %reduce-scatter.5.cloned.1.call-done = f32[32,4096]{1,0:T(8,128)} async-done(((f32[512,4096]{1,0:T(8,128)}), f32[32,4096]{1,0:T(8,128)}) %reduce-scatter.5.cloned.1.call-update) | async-done | bytes 524304 | tf_op jit(solution)/shard_map/reduce_scatter | solution.py:80
  648.7 0.0 copy-done.2
  648.7 0.0 copy-done.3
  648.7 0.0 copy-done.4
  648.7 2.4 divide_subtract_fusion
  (5 shorter events, 0.0 us)
Async XLA Ops:
  7.2 79.3 %all-gather.4.cloned.1.call-start = ((), (), s32[]{:S(2)}) async-start(), calls=%async_computation.2 | async-start | bytes 3342336 | tf_op jit(solution)/shard_map/all_gather | solution.py:45
  7.9 139.9 %all-gather.6.cloned.1.call-start = ((), (), s32[]{:S(2)}) async-start(), calls=%async_computation.3 | async-start | bytes 4456448 | tf_op jit(solution)/shard_map/all_gather | solution.py:47
  9.7 292.7 %all-reduce.3.cloned.1.call-start = ((), (), s32[]{:S(2)}) async-start(), calls=%async_computation.4 | async-start | bytes 6291456 | tf_op jit(solution)/shard_map/psum | solution.py:57
  147.8 6.1 copy-start.9
  153.9 3.7 copy-start.5
  153.9 148.6 %copy-start = (bf16[384,4096]{1,0:T(8,128)(2,1)S(1)}, bf16[384,4096]{1,0:T(8,128)(2,1)}, u32[]{:S(2)}) copy-start(bf16[384,4096]{1,0:T(8,128)(2,1)} %all-gather.4.cloned.1.call-done) | copy-start | bytes 9437188
  157.5 299.2 %all-reduce.5.cloned.1.call-start = ((), (), s32[]{:S(2)}) async-start(), calls=%async_computation.5 | async-start | bytes 6291456 | tf_op jit(solution)/shard_map/psum | solution.py:64
  312.2 223.2 %reduce-scatter.7.cloned.1.call-start = ((), (), s32[]{:S(2)}) async-start(), calls=%async_computation.7 | async-start | bytes 278528
  456.7 4.7 copy-start.10
  456.7 4.7 copy-start.11
  461.4 2.7 copy-start.1
  465.0 183.7 %reduce-scatter.5.cloned.1.call-start = ((), (), s32[]{:S(2)}) async-start(), calls=%async_computation.6 | async-start | bytes 8912896 | tf_op jit(solution)/shard_map/reduce_scatter | solution.py:80
  474.0 62.2 %copy-start.6 = (f32[2,32]{1,0:T(2,128)S(1)}, f32[2,32]{1,0:T(2,128)}, u32[]{:S(2)}) copy-start(f32[2,32]{1,0:T(2,128)} %param.13) | copy-start | bytes 772
  474.0 62.2 %copy-start.7 = (f32[2,32]{1,0:T(2,128)S(1)}, f32[2,32]{1,0:T(2,128)}, u32[]{:S(2)}) copy-start(f32[2,32]{1,0:T(2,128)} %param.16) | copy-start | bytes 772
  474.0 62.2 %copy-start.8 = (f32[2,32]{1,0:T(2,128)S(1)}, f32[2,32]{1,0:T(2,128)}, u32[]{:S(2)}) copy-start(f32[2,32]{1,0:T(2,128)} %param.17) | copy-start | bytes 772
  474.0 174.7 %copy-start.2 = (f32[32,4096]{1,0:T(8,128)S(1)}, f32[32,4096]{1,0:T(8,128)}, u32[]{:S(2)}) copy-start(f32[32,4096]{1,0:T(8,128)} %param.12) | copy-start | bytes 1572868
  474.0 174.7 %copy-start.3 = (f32[32,4096]{1,0:T(8,128)S(1)}, f32[32,4096]{1,0:T(8,128)}, u32[]{:S(2)}) copy-start(f32[32,4096]{1,0:T(8,128)} %param.14) | copy-start | bytes 1572868
  474.0 174.7 %copy-start.4 = (f32[32,4096]{1,0:T(8,128)S(1)}, f32[32,4096]{1,0:T(8,128)}, u32[]{:S(2)}) copy-start(f32[32,4096]{1,0:T(8,128)} %param.15) | copy-start | bytes 1572868
Sparse Core Ops, SparseCore 0:
  9.8 76.6 all-gather.3
  89.8 57.9 all-gather.5
  157.6 144.8 all-reduce.2
  312.4 144.3 all-reduce.4
  465.1 70.2 reduce-scatter.6
  539.8 108.8 reduce-scatter.4
where the time goes:
time: 659 us; the launch traced here: 658 us
  waiting for transfers between devices  577 us (88%)
  matrix products  30.8 us (5%)
  blocking collectives  23.4 us (4%)
  between operations  14.2 us (2%)
  other arithmetic  10.7 us (2%)
    psum x1, waiting for transfers between devices, body(): lax.psum(jnp.dot(scaled, weight_slab, preferred_element_type=jnp.float32)...  145 us
    psum x1, waiting for transfers between devices, body(): lax.psum(jnp.dot(dual_scaled, dual_weight, preferred_element_type=jnp.flo...  144 us
    reduce_scatter x1, waiting for transfers between devices, body(): lax.psum_scatter(grad_slab, 'rep', scatter_dimension=0, tiled=True)  111 us
    unnamed x7, waiting for transfers between devices  62.1 us
    all_gather x1, waiting for transfers between devices, body(): lax.all_gather(map_weight.astype(jnp.bfloat16), 'rep', axis=0, tiled=True)  61.3 us
    all_gather x1, waiting for transfers between devices, body(): group_rows = lax.all_gather(samples, 'fsdp', axis=0, tiled=True)  52.4 us
    all_gather x1, blocking collectives, body(): lax.all_gather(map_vector.astype(jnp.bfloat16), 'rep', axis=1, tiled=True)  23.4 us
  transfers between devices with their start and end apart: 6, of which 6 were waited for; matrix products, arithmetic and copies ran while one was open for 2% of the time, Pallas kernels for 0%

commit v1 on v0

v1 whole, which is shorter than its diff:
```python
import jax
import jax.numpy as jnp
from jax import lax
from jax.sharding import Mesh, PartitionSpec as P

beta_one = 0.9
beta_two = 0.999
learn_rate = 0.001
epsilon = 1e-08
adam_step = 10
extra = 128

flip = [(0, 1), (1, 0)]


def contract_last(left, right):
    return lax.dot_general(
        left, right, (((1,), (1,)), ((), ())), preferred_element_type=jnp.float32
    )


def contract_first(left, right):
    return lax.dot_general(
        left, right, (((0,), (0,)), ((), ())), preferred_element_type=jnp.float32
    )


def dot(left, right):
    return jnp.dot(left, right, preferred_element_type=jnp.float32)


def adam_update(param, grad, moment, square):
    moment_new = beta_one * moment + (1.0 - beta_one) * grad
    square_new = beta_two * square + (1.0 - beta_two) * grad * grad
    fix_one = 1.0 - beta_one**adam_step
    fix_two = 1.0 - beta_two**adam_step
    update = learn_rate * (moment_new / fix_one) / (jnp.sqrt(square_new / fix_two) + epsilon)
    return (param - update, moment_new, square_new)


def shift_y(value, step):
    return lax.ppermute(value, "y", [(i, (i + step) % 4) for i in range(4)])


ring_x = (0, 2, 1, 3)


def shift_x(value, step):
    return lax.ppermute(
        value, ("xl", "xh"), [(ring_x[i], ring_x[(i + step) % 4]) for i in range(4)]
    )


def spread(value, shift):
    return jnp.concatenate([value] + [shift(value, step) for step in (1, 2, 3)], axis=0)


def collect(value, shift):
    rows = value.shape[0] // 4
    total = value[:rows].astype(jnp.float32)
    for step in (1, 2, 3):
        piece = shift(value[rows * step : rows * (step + 1)], -step)
        total = total + piece.astype(jnp.float32)
    return total


def other_core(value):
    return lax.ppermute(value, "core", flip)


def body(
    samples,
    dual_weight,
    dual_vector,
    map_weight,
    map_vector,
    moment_weight,
    square_weight,
    moment_vector,
    square_vector,
):
    core = lax.axis_index("core")
    width = samples.shape[1]
    inverse_rows = 1.0 / 6144

    packed = jnp.concatenate(
        [
            map_weight.astype(jnp.bfloat16),
            jnp.pad(map_vector.astype(jnp.bfloat16).T, ((0, 0), (0, extra - 2))),
        ],
        axis=1,
    )
    first = spread(spread(packed[:16], shift_x), shift_y)
    second = spread(spread(packed[16:], shift_y), shift_x)
    slab = jnp.concatenate([first, second], axis=0)
    weight = slab[:, :width]
    readout = slab[:, width].astype(jnp.float32)
    offset = slab[:, width + 1].astype(jnp.float32)

    rows_own = lax.all_gather(samples, "z", axis=0, tiled=True)
    rows_other = other_core(rows_own)

    half = dual_weight.shape[0] // 2
    dual_half = lax.dynamic_slice_in_dim(dual_weight, core * half, half, axis=0)
    dual_small = lax.dynamic_slice_in_dim(dual_vector, core * half, half, axis=1)
    dual_slab = jnp.concatenate([dual_half, lax.ppermute(dual_half, "xl", flip)], axis=0)
    dual_pair = jnp.concatenate([dual_small, lax.ppermute(dual_small, "xl", flip)], axis=1)

    def reduce_rows(left_own, left_other, right):
        sent = other_core(dot(left_other, right).astype(jnp.bfloat16))
        both = dot(left_own, right).astype(jnp.bfloat16).astype(jnp.float32) + sent.astype(
            jnp.float32
        )
        return lax.psum_scatter(
            both.astype(jnp.bfloat16), "z", scatter_dimension=0, tiled=True
        ).astype(jnp.float32)

    sigma_own = jax.nn.sigmoid(contract_last(rows_own, weight) + offset)
    sigma_other = jax.nn.sigmoid(contract_last(rows_other, weight) + offset)
    scaled_own = (readout * sigma_own).astype(jnp.bfloat16)
    scaled_other = (readout * sigma_other).astype(jnp.bfloat16)

    sample_float = samples.astype(jnp.float32)
    mapped = sample_float + reduce_rows(scaled_own, scaled_other, weight)
    low_own = lax.all_gather(mapped.astype(jnp.bfloat16), "z", axis=0, tiled=True)
    low_other = other_core(low_own)

    def dual_of(low):
        hidden = contract_last(low, dual_slab) + dual_pair[1]
        return (dual_pair[0] * jax.nn.sigmoid(hidden)).astype(jnp.bfloat16)

    dual_grad = mapped + reduce_rows(dual_of(low_own), dual_of(low_other), dual_slab)
    residual = (sample_float - dual_grad).astype(jnp.bfloat16)
    residual_own = lax.all_gather(residual, "z", axis=0, tiled=True)
    residual_other = other_core(residual_own)

    def curve_of(sigma, rows):
        pulled = contract_last(rows, weight)
        curve = readout * (sigma * (1.0 - sigma)) * pulled
        sums = jnp.stack([jnp.sum(sigma * pulled, axis=0), jnp.sum(curve, axis=0)], axis=1)
        return curve.astype(jnp.bfloat16), sums

    curve_own, sums_own = curve_of(sigma_own, residual_own)
    curve_other, sums_other = curve_of(sigma_other, residual_other)
    left_stack = jnp.concatenate([scaled_own, scaled_other, curve_own, curve_other], axis=0)
    right_stack = jnp.concatenate(
        [residual_own, residual_other, rows_own, rows_other], axis=0
    )
    grad_slab = (contract_first(left_stack, right_stack) * inverse_rows).astype(jnp.bfloat16)
    grad_small = ((sums_own + sums_other) * inverse_rows).astype(jnp.bfloat16)
    grad = jnp.concatenate(
        [grad_slab, jnp.pad(grad_small, ((0, 0), (0, extra - 2)))], axis=1
    )
    count = grad.shape[0] // 2
    grad_first = collect(collect(grad[:count], shift_y).astype(jnp.bfloat16), shift_x)
    grad_second = collect(collect(grad[count:], shift_x).astype(jnp.bfloat16), shift_y)
    owner = jnp.concatenate([grad_first, grad_second], axis=0)
    owner_weight = owner[:, :width]
    owner_vector = owner[:, width : width + 2].T

    next_weight, next_moment_weight, next_square_weight = adam_update(
        map_weight, owner_weight, moment_weight, square_weight
    )
    raw_vector, next_moment_vector, next_square_vector = adam_update(
        map_vector, owner_vector, moment_vector, square_vector
    )
    next_vector = jnp.concatenate([jnp.maximum(raw_vector[0:1], 0.0), raw_vector[1:2]], axis=0)
    return (
        next_weight,
        next_vector,
        next_moment_weight,
        next_square_weight,
        next_moment_vector,
        next_square_vector,
    )


def solution(mesh):
    fsdp = ("xl", "z")
    rep = ("y", "xh", "core")
    fine = Mesh(mesh.devices.reshape(2, 8, 4, 2, 2), fsdp + rep)
    rows = P(fsdp + rep, None)
    columns = P(None, fsdp + rep)
    return jax.shard_map(
        body,
        mesh=fine,
        in_specs=(rows, P(fsdp, None), P(None, fsdp), rows, columns, rows, rows, columns, columns),
        out_specs=(rows, columns, rows, rows, columns, columns),
        check_vma=False,
    )
```

time: 659 us -> 333 us (0.51)
  waiting for transfers between devices: 577 us -> 222 us
  starting transfers between devices: 0.42 us -> 36.4 us
  blocking collectives: 23.4 us -> 0 us
  local copies, waits for them, and re-layouts: 1.8 us -> 12.8 us
  matrix products: 30.8 us -> 37.4 us
    psum x2 -> x0, waiting for transfers between devices: 289 us -> none  [the longest x1 145 us: body(): lax.psum(jnp.dot(scaled, weight_slab, preferred_element_type=jnp.float32)...]
    unnamed x7 -> x5, waiting for transfers between devices: 62.1 us -> 0.08 us
    ppermute x0 -> x31, waiting for transfers between devices: none -> 61 us  [the longest x12 39 us: shift_y(): return lax.ppermute(value, 'y', [(i, (i + step) % 4) for i in range(4)])]
    ppermute x0 -> x31, starting transfers between devices: none -> 36.2 us  [the longest x12 20.5 us: shift_y(): return lax.ppermute(value, 'y', [(i, (i + step) % 4) for i in range(4)])]
    reduce_scatter x1 -> x2, waiting for transfers between devices: 111 us -> 79.2 us  [reduce_rows(): lax.psum_scatter(both.astype(jnp.bfloat16), 'z', scatter_dimension=0, til...]
    all_gather x2 -> x3, waiting for transfers between devices: 114 us -> 82.1 us  [the longest x1 39.1 us: body(): residual_own = lax.all_gather(residual, 'z', axis=0, tiled=True)]
    all_gather x1 -> x0, blocking collectives: 23.4 us -> none  [body(): lax.all_gather(map_vector.astype(jnp.bfloat16), 'rep', axis=1, tiled=True)]
    unnamed x27 -> x45, local copies, waits for them, and re-layouts: 1.79 us -> 9.26 us
  transfers between devices with their start and end apart: 6 -> 36, of which waited for: 6 -> 17; matrix products, arithmetic and copies ran while one was open for 2% -> 6% of each run, Pallas kernels for 0% -> 0%
where the time goes in v1:
time: 333 us
  waiting for transfers between devices  222 us (67%)
  matrix products  37.4 us (11%)
  starting transfers between devices  36.4 us (11%)
  between operations  14.1 us (4%)
  local copies, waits for them, and re-layouts  12.8 us (4%)
  other arithmetic  10.1 us (3%)
    reduce_scatter x2, waiting for transfers between devices, reduce_rows(): lax.psum_scatter(both.astype(jnp.bfloat16), 'z', scatter_dimension=0, til...  79.2 us
    all_gather x1, waiting for transfers between devices, body(): residual_own = lax.all_gather(residual, 'z', axis=0, tiled=True)  39.1 us
    ppermute x12, waiting for transfers between devices, shift_y(): return lax.ppermute(value, 'y', [(i, (i + step) % 4) for i in range(4)])  39 us
    all_gather x1, waiting for transfers between devices, body(): lax.all_gather(mapped.astype(jnp.bfloat16), 'z', axis=0, tiled=True)  36.9 us
    ppermute x12, starting transfers between devices, shift_y(): return lax.ppermute(value, 'y', [(i, (i + step) % 4) for i in range(4)])  20.5 us
    dot_general x4, matrix products, dot(): return jnp.dot(left, right, preferred_element_type=jnp.float32)  16.6 us
    dot_general x4, matrix products, contract_last(): lax.dot_general(left, right, (((1,), (1,)), ((), ())), preferred_element_...  15.4 us
    ppermute x12, starting transfers between devices, shift_x(): lax.ppermute(value, ('xl', 'xh'), [(ring_x[i], ring_x[(i + step) % 4]) fo...  14 us
  transfers between devices with their start and end apart: 36, of which 17 were waited for; matrix products, arithmetic and copies ran while one was open for 6% of the time, Pallas kernels for 0%

profile of v1, /device:TPU:2, one launch (start us, length us, event | category | flops | bytes accessed | tf_op | source)
XLA Modules:
  0.0 333.2 jit_solution(8314518129349962806)
XLA Ops:
  7.2 0.7 convert_bitcast_fusion
  8.0 1.1 convert_element_type.153
  9.1 0.7 fusion.118
  9.8 1.5 collective-permute-start
  11.3 2.8 collective-permute-start.1
  14.6 1.6 collective-permute-start.6
  16.1 2.9 collective-permute-start.7
  19.1 1.4 collective-permute-start.8
  20.6 1.2 collective-permute-start.3
  21.8 2.9 collective-permute-start.4
  24.7 1.3 collective-permute-start.5
  26.1 1.4 collective-permute-start.9
  27.4 2.3 collective-permute-start.10
  29.8 0.7 constant_dynamic-update-slice_fusion.12
  30.4 0.7 constant_dynamic-update-slice_fusion.11
  31.8 6.0 %collective-permute-done.3 = bf16[64,4224]{1,0:T(8,128)(2,1)S(1)} collective-permute-done((bf16[64,4224]{1,0:T(8,128)(2,1)S(1)}, bf16[64,4224]{1,0:T(8,128)(2,1)S(1)}, u32[]{:S(2)}, u32[]{:S(2)}) %collective-permute-start.3) | collective-permute-done | bytes 540704 | tf_op jit(solution)/shard_map/ppermute | solution.py:42
  37.9 0.9 constant_dynamic-update-slice_fusion.9
  38.8 8.8 %collective-permute-done.4 = bf16[64,4224]{1,0:T(8,128)(2,1)S(1)} collective-permute-done((bf16[64,4224]{1,0:T(8,128)(2,1)S(1)}, bf16[64,4224]{1,0:T(8,128)(2,1)S(1)}, u32[]{:S(2)}, u32[]{:S(2)}) %collective-permute-start.4) | collective-permute-done | bytes 540704 | tf_op jit(solution)/shard_map/ppermute | solution.py:42
  47.6 0.9 constant_dynamic-update-slice_fusion.8
  48.5 0.8 constant_dynamic-update-slice_fusion.7
  49.3 0.7 constant_dynamic-update-slice_fusion.6
  49.9 0.7 constant_dynamic-update-slice_fusion.5
  51.3 0.7 constant_dynamic-update-slice_fusion.3
  51.9 0.8 constant_dynamic-update-slice_fusion.2
  52.8 6.1 %all-gather.4.cloned.1.call-done = bf16[192,4096]{1,0:T(8,128)(2,1)} async-done(((bf16[24,4096]{1,0:T(8,128)(2,1)}), bf16[192,4096]{1,0:T(8,128)(2,1)}) %all-gather.4.cloned.1.call-update) | async-done | bytes 1572880 | tf_op jit(solution)/shard_map/all_gather | solution.py:100
  58.9 0.8 constant_dynamic-update-slice_fusion.1
  59.7 0.8 constant_dynamic-update-slice_fusion
  60.5 1.3 convert_reduce_fusion.1
  61.9 4.3 %fusion.70 = f32[192,512]{1,0:T(8,128)S(1)} fusion(bf16[192,4096]{1,0:T(8,128)(2,1)} %all-gather.4.cloned.1.call-done, bf16[512,4224]{1,0:T(8,128)(2,1)} %constant_dynamic-update-slice_fusion, f32[512]{0:T(512)S(1)} %get-tuple-element.31), kind=kOutput, calls=%fused_computation.57 | convolution fusion | flops 805699584 | bytes 6162432 | tf_op jit(solution)/shard_map/dot_general | solution.py:17
  66.2 2.3 multiply_convert_fusion.1
  68.6 1.0 convolution_convert_fusion.2
  70.2 3.0 collective-permute-done.13
  73.2 2.2 fusion.13
  75.5 39.1 %reduce-scatter.3.cloned.1.call-done = bf16[24,4096]{1,0:T(8,128)(2,1)} async-done(((bf16[192,4096]{1,0:T(8,128)(2,1)}), bf16[24,4096]{1,0:T(8,128)(2,1)}) %reduce-scatter.3.cloned.1.call-update) | async-done | bytes 196624 | tf_op jit(solution)/shard_map/reduce_scatter | solution.py:114
  114.6 1.7 fusion.88
  116.3 1.7 constant_dynamic-slice_fusion
  118.6 36.9 %all-gather.6.cloned.1.call-done = bf16[192,4096]{1,0:T(8,128)(2,1)} async-done(((bf16[24,4096]{1,0:T(8,128)(2,1)}), bf16[192,4096]{1,0:T(8,128)(2,1)}) %all-gather.6.cloned.1.call-update) | async-done | bytes 1572880 | tf_op jit(solution)/shard_map/all_gather | solution.py:125
  156.1 5.5 %collective-permute-done.14 = f32[2,256]{1,0:T(2,128)S(1)} collective-permute-done((f32[2,256]{1,0:T(2,128)S(1)}, f32[2,256]{1,0:T(2,128)S(1)}, u32[]{:S(2)}, u32[]{:S(2)}) %collective-permute-start.14) | collective-permute-done | bytes 2080 | tf_op jit(solution)/shard_map/ppermute | solution.py:107
  161.6 6.5 %convolution_convert_fusion = bf16[192,4096]{1,0:T(8,128)(2,1)} fusion(bf16[192,4096]{1,0:T(8,128)(2,1)} %collective-permute-done.16, bf16[256,4096]{1,0:T(8,128)(2,1)} %collective-permute-done.15, bf16[256,4096]{1,0:T(8,128)(2,1)S(1)} %constant_dynamic-slice_fusion, f32[512]{0:T(512)S(1)} %bitcast.35, f32[512]{0:T(512)S(1)} %bitcast.33), kind=kOutput, calls=%fused_computation.10 | convolution fusion | flops 1628766208 | bytes 7344128 | tf_op jit(solution)/shard_map/dot_general | solution.py:29
  168.1 3.7 %collective-permute-done.17 = bf16[192,4096]{1,0:T(8,128)(2,1)} collective-permute-done((bf16[192,4096]{1,0:T(8,128)(2,1)}, bf16[192,4096]{1,0:T(8,128)(2,1)}, u32[]{:S(2)}, u32[]{:S(2)}) %collective-permute-start.17) | collective-permute-done | bytes 1572896 | tf_op jit(solution)/shard_map/ppermute | solution.py:68
  171.8 7.0 %fusion.10 = bf16[192,4096]{1,0:T(8,128)(2,1)} fusion(bf16[192,4096]{1,0:T(8,128)(2,1)} %collective-permute-done.17, bf16[256,4096]{1,0:T(8,128)(2,1)} %collective-permute-done.15, bf16[256,4096]{1,0:T(8,128)(2,1)S(1)} %constant_dynamic-slice_fusion, bf16[192,4096]{1,0:T(8,128)(2,1)} %all-gather.6.cloned.1.call-done, f32[512]{0:T(512)S(1)} %bitcast.36, ...), kind=kOutput, calls=%fused_computation.14 | convolution fusion | flops 1631911936 | bytes 8916992 | tf_op jit(solution)/shard_map/dot_general | solution.py:29
  178.9 40.1 %reduce-scatter.5.cloned.1.call-done = bf16[24,4096]{1,0:T(8,128)(2,1)} async-done(((bf16[192,4096]{1,0:T(8,128)(2,1)}), bf16[24,4096]{1,0:T(8,128)(2,1)}) %reduce-scatter.5.cloned.1.call-update) | async-done | bytes 196624 | tf_op jit(solution)/shard_map/reduce_scatter | solution.py:114
  219.0 1.7 fusion.83
  220.7 39.1 %all-gather.8.cloned.1.call-done = bf16[192,4096]{1,0:T(8,128)(2,1)} async-done(((bf16[24,4096]{1,0:T(8,128)(2,1)}), bf16[192,4096]{1,0:T(8,128)(2,1)}) %all-gather.8.cloned.1.call-update) | async-done | bytes 1572880 | tf_op jit(solution)/shard_map/all_gather | solution.py:134
  259.9 4.2 %fusion.17 = f32[192,512]{1,0:T(8,128)S(1)} fusion(bf16[192,4096]{1,0:T(8,128)(2,1)} %all-gather.8.cloned.1.call-done, bf16[512,4224]{1,0:T(8,128)(2,1)} %constant_dynamic-update-slice_fusion), kind=kOutput, calls=%fused_computation.24 | convolution fusion | flops 805306368 | bytes 6160384 | tf_op jit(solution)/shard_map/dot_general | solution.py:17
  264.1 4.5 %multiply_reduce_fusion = (f32[512]{0:T(512)S(1)}, f32[512]{0:T(512)S(1)}, bf16[192,512]{1,0:T(8,128)(2,1)S(1)}, bf16[192,512]{1,0:T(8,128)(2,1)S(1)}, f32[512]{0:T(512)S(1)}, /*index=5*/f32[512]{0:T(512)S(1)}) fusion(f32[192,512]{1,0:T(8,128)S(1)} %copy-done.12, f32[512]{0:T(512)S(1)} %get-tuple-element.30, f32[192,512]{1,0:T(8,128)S(1)} %fusion.17, ...), kind=kOutput, calls=%fused_computation.87 | convolution fusion | flops 806877184 | bytes 7350272 | tf_op jit(solution)/shard_map/dot_general | solution.py:17
  268.8 5.4 %multiply_convert_fusion = bf16[512,4096]{1,0:T(8,128)(2,1)S(1)} fusion(bf16[192,4096]{1,0:T(8,128)(2,1)} %copy-done.10, bf16[192,4096]{1,0:T(8,128)(2,1)S(1)} %copy-done.9, bf16[192,4096]{1,0:T(8,128)(2,1)} %copy-done.11, bf16[192,4096]{1,0:T(8,128)(2,1)} %all-gather.8.cloned.1.call-done, bf16[192,512]{1,0:T(8,128)(2,1)S(1)} %get-tuple-element.51, ...), kind=kOutput, calls=%fused_computation.2 | convolution fusion | flops 3253731328 | bytes 11272192 | tf_op jit(solution)/shard_map/dot_general | solution.py:23
  274.9 1.6 collective-permute-start.21
  276.4 2.7 collective-permute-start.20
  279.2 1.4 collective-permute-start.19
  280.6 1.5 collective-permute-start.27
  282.1 1.2 collective-permute-start.26
  283.2 7.6 %collective-permute-done.21 = bf16[64,4224]{1,0:T(8,128)(2,1)S(1)} collective-permute-done((bf16[64,4224]{1,0:T(8,128)(2,1)S(1)}, bf16[64,4224]{1,0:T(8,128)(2,1)S(1)}, u32[]{:S(2)}, u32[]{:S(2)}) %collective-permute-start.21) | collective-permute-done | bytes 540704 | tf_op jit(solution)/shard_map/ppermute | solution.py:42
  291.5 11.9 %collective-permute-done.20 = bf16[64,4224]{1,0:T(8,128)(2,1)S(1)} collective-permute-done((bf16[64,4224]{1,0:T(8,128)(2,1)S(1)}, bf16[64,4224]{1,0:T(8,128)(2,1)S(1)}, u32[]{:S(2)}, u32[]{:S(2)}) %collective-permute-start.20) | collective-permute-done | bytes 540704 | tf_op jit(solution)/shard_map/ppermute | solution.py:42
  303.4 5.3 %collective-permute-done.25 = bf16[64,4224]{1,0:T(8,128)(2,1)S(1)} collective-permute-done((bf16[64,4224]{1,0:T(8,128)(2,1)S(1)}, bf16[64,4224]{1,0:T(8,128)(2,1)S(1)}, u32[]{:S(2)}, u32[]{:S(2)}) %collective-permute-start.25) | collective-permute-done | bytes 540704 | tf_op jit(solution)/shard_map/ppermute | solution.py:49
  309.3 0.7 collective-permute-start.30
  309.9 1.2 collective-permute-start.29
  311.1 1.6 collective-permute-start.28
  312.7 0.7 collective-permute-start.24
  313.4 1.5 collective-permute-start.23
  314.9 4.1 %collective-permute-done.30 = bf16[16,4224]{1,0:T(8,128)(2,1)S(1)} collective-permute-done((bf16[16,4224]{1,0:T(8,128)(2,1)S(1)}, bf16[16,4224]{1,0:T(8,128)(2,1)S(1)}, u32[]{:S(2)}, u32[]{:S(2)}) %collective-permute-start.30) | collective-permute-done | bytes 135200 | tf_op jit(solution)/shard_map/ppermute | solution.py:42
  319.6 1.1 collective-permute-done.23
  320.8 3.2 collective-permute-done.22
  324.7 1.3 divide_subtract_fusion
  (94 shorter events, 8.3 us)
Async XLA Ops:
  7.2 148.3 %copy-start = (f32[2,512]{1,0:T(2,128)S(1)}, f32[2,512]{1,0:T(2,128)}, u32[]{:S(2)}) copy-start(f32[2,512]{1,0:T(2,128)} %param.11) | copy-start | bytes 12292
  7.2 51.7 %all-gather.4.cloned.1.call-start = ((), (), s32[]{:S(2)}) async-start(), calls=%async_computation.2 | async-start | bytes 1769472 | tf_op jit(solution)/shard_map/all_gather | solution.py:100
  9.8 9.3 %collective-permute-start = (bf16[16,4224]{1,0:T(8,128)(2,1)S(1)}, bf16[16,4224]{1,0:T(8,128)(2,1)S(1)}, u32[]{:S(2)}, u32[]{:S(2)}) collective-permute-start(bf16[16,4224]{1,0:T(8,128)(2,1)S(1)} %get-tuple-element.60), channel_id=1, source_target_pairs={{0,128},{128,2},{2,130},{130,0},{1,129},{129,3},{3,131},{131,1},{4... | collective-permute-start | bytes 405512 | tf_op jit(solution)/shard_map/ppermute | solution.py:49
  11.3 9.3 %collective-permute-start.1 = (bf16[16,4224]{1,0:T(8,128)(2,1)S(1)}, bf16[16,4224]{1,0:T(8,128)(2,1)S(1)}, u32[]{:S(2)}, u32[]{:S(2)}) collective-permute-start(bf16[16,4224]{1,0:T(8,128)(2,1)S(1)} %get-tuple-element.60), channel_id=1, source_target_pairs={{0,2},{128,130},{2,0},{130,128},{1,3},{129,131},{3,1},{131,129},{4... | collective-permute-start | bytes 405512 | tf_op jit(solution)/shard_map/ppermute | solution.py:49
  14.1 6.4 %collective-permute-start.2 = (bf16[16,4224]{1,0:T(8,128)(2,1)S(1)}, bf16[16,4224]{1,0:T(8,128)(2,1)S(1)}, u32[]{:S(2)}, u32[]{:S(2)}) collective-permute-start(bf16[16,4224]{1,0:T(8,128)(2,1)S(1)} %get-tuple-element.60), channel_id=1, source_target_pairs={{0,130},{128,0},{2,128},{130,2},{1,131},{129,1},{3,129},{131,3},{4... | collective-permute-start | bytes 405512 | tf_op jit(solution)/shard_map/ppermute | solution.py:49
  14.6 10.1 %collective-permute-start.6 = (bf16[16,4224]{1,0:T(8,128)(2,1)S(1)}, bf16[16,4224]{1,0:T(8,128)(2,1)S(1)}, u32[]{:S(2)}, u32[]{:S(2)}) collective-permute-start(bf16[16,4224]{1,0:T(8,128)(2,1)S(1)} %get-tuple-element.58), channel_id=1, source_target_pairs={{0,4},{4,8},{8,12},{12,0},{1,5},{5,9},{9,13},{13,1},{2,6},{6,10},{... | collective-permute-start | bytes 405512 | tf_op jit(solution)/shard_map/ppermute | solution.py:42
  16.1 9.9 %collective-permute-start.7 = (bf16[16,4224]{1,0:T(8,128)(2,1)S(1)}, bf16[16,4224]{1,0:T(8,128)(2,1)S(1)}, u32[]{:S(2)}, u32[]{:S(2)}) collective-permute-start(bf16[16,4224]{1,0:T(8,128)(2,1)S(1)} %get-tuple-element.58), channel_id=1, source_target_pairs={{0,8},{4,12},{8,0},{12,4},{1,9},{5,13},{9,1},{13,5},{2,10},{6,14},... | collective-permute-start | bytes 405512 | tf_op jit(solution)/shard_map/ppermute | solution.py:42
  19.1 95.5 %reduce-scatter.3.cloned.1.call-start = ((), (), s32[]{:S(2)}) async-start(), calls=%async_computation.3 | async-start | bytes 1769472 | tf_op jit(solution)/shard_map/reduce_scatter | solution.py:114
  19.1 6.9 %collective-permute-start.8 = (bf16[16,4224]{1,0:T(8,128)(2,1)S(1)}, bf16[16,4224]{1,0:T(8,128)(2,1)S(1)}, u32[]{:S(2)}, u32[]{:S(2)}) collective-permute-start(bf16[16,4224]{1,0:T(8,128)(2,1)S(1)} %get-tuple-element.58), channel_id=1, source_target_pairs={{0,12},{4,0},{8,4},{12,8},{1,13},{5,1},{9,5},{13,9},{2,14},{6,2},{... | collective-permute-start | bytes 405512 | tf_op jit(solution)/shard_map/ppermute | solution.py:42
  20.6 17.2 %collective-permute-start.3 = (bf16[64,4224]{1,0:T(8,128)(2,1)S(1)}, bf16[64,4224]{1,0:T(8,128)(2,1)S(1)}, u32[]{:S(2)}, u32[]{:S(2)}) collective-permute-start(bf16[64,4224]{1,0:T(8,128)(2,1)S(1)} %pad_maximum_fusion.7), channel_id=1, source_target_pairs={{0,4},{4,8},{8,12},{12,0},{1,5},{5,9},{9,13},{13,1},{2,6},{6,10},{... | collective-permute-start | bytes 1622024 | tf_op jit(solution)/shard_map/ppermute | solution.py:42
  21.8 25.8 %collective-permute-start.4 = (bf16[64,4224]{1,0:T(8,128)(2,1)S(1)}, bf16[64,4224]{1,0:T(8,128)(2,1)S(1)}, u32[]{:S(2)}, u32[]{:S(2)}) collective-permute-start(bf16[64,4224]{1,0:T(8,128)(2,1)S(1)} %pad_maximum_fusion.7), channel_id=1, source_target_pairs={{0,8},{4,12},{8,0},{12,4},{1,9},{5,13},{9,1},{13,5},{2,10},{6,14},... | collective-permute-start | bytes 1622024 | tf_op jit(solution)/shard_map/ppermute | solution.py:42
  24.7 23.8 %collective-permute-start.5 = (bf16[64,4224]{1,0:T(8,128)(2,1)S(1)}, bf16[64,4224]{1,0:T(8,128)(2,1)S(1)}, u32[]{:S(2)}, u32[]{:S(2)}) collective-permute-start(bf16[64,4224]{1,0:T(8,128)(2,1)S(1)} %pad_maximum_fusion.7), channel_id=1, source_target_pairs={{0,12},{4,0},{8,4},{12,8},{1,13},{5,1},{9,5},{13,9},{2,14},{6,2},{... | collective-permute-start | bytes 1622024 | tf_op jit(solution)/shard_map/ppermute | solution.py:42
  26.1 25.9 %collective-permute-start.9 = (bf16[64,4224]{1,0:T(8,128)(2,1)S(1)}, bf16[64,4224]{1,0:T(8,128)(2,1)S(1)}, u32[]{:S(2)}, u32[]{:S(2)}) collective-permute-start(bf16[64,4224]{1,0:T(8,128)(2,1)S(1)} %pad_maximum_fusion.8), channel_id=1, source_target_pairs={{0,128},{128,2},{2,130},{130,0},{1,129},{129,3},{3,131},{131,1},{4... | collective-permute-start | bytes 1622024 | tf_op jit(solution)/shard_map/ppermute | solution.py:49
  27.4 31.4 %collective-permute-start.10 = (bf16[64,4224]{1,0:T(8,128)(2,1)S(1)}, bf16[64,4224]{1,0:T(8,128)(2,1)S(1)}, u32[]{:S(2)}, u32[]{:S(2)}) collective-permute-start(bf16[64,4224]{1,0:T(8,128)(2,1)S(1)} %pad_maximum_fusion.8), channel_id=1, source_target_pairs={{0,2},{128,130},{2,0},{130,128},{1,3},{129,131},{3,1},{131,129},{4... | collective-permute-start | bytes 1622024 | tf_op jit(solution)/shard_map/ppermute | solution.py:49
  37.8 21.9 %collective-permute-start.11 = (bf16[64,4224]{1,0:T(8,128)(2,1)S(1)}, bf16[64,4224]{1,0:T(8,128)(2,1)S(1)}, u32[]{:S(2)}, u32[]{:S(2)}) collective-permute-start(bf16[64,4224]{1,0:T(8,128)(2,1)S(1)} %pad_maximum_fusion.8), channel_id=1, source_target_pairs={{0,130},{128,0},{2,128},{130,2},{1,131},{129,1},{3,129},{131,3},{4... | collective-permute-start | bytes 1622024 | tf_op jit(solution)/shard_map/ppermute | solution.py:49
  58.9 7.3 %collective-permute-start.12 = (bf16[192,4096]{1,0:T(8,128)(2,1)}, bf16[192,4096]{1,0:T(8,128)(2,1)S(1)}, u32[]{:S(2)}, u32[]{:S(2)}) collective-permute-start(bf16[192,4096]{1,0:T(8,128)(2,1)} %all-gather.4.cloned.1.call-done), channel_id=1, source_target_pairs={{0,1},{1,0},{2,3},{3,2},{4,5},{5,4},{6,7},{7,6},{8,9},{9,8},{10,11... | collective-permute-start | bytes 4718600 | tf_op jit(solution)/shard_map/ppermute | solution.py:68
  60.5 5.7 %slice-start = ((s8[4325376]{0:T(1024)(128)(4,1)}), s8[4194304]{0:T(1024)(128)(4,1)S(1)}, s32[]{:S(2)}) async-start(s8[4325376]{0:T(1024)(128)(4,1)} %bitcast.27), calls=%async_computation.7 | async-start | bytes 8388608
  61.9 4.4 %slice-start.1 = ((s8[4325376]{0:T(1024)(128)(4,1)}), s8[131072]{0:T(1024)(128)(4,1)S(1)}, s32[]{:S(2)}) async-start(s8[4325376]{0:T(1024)(128)(4,1)} %bitcast.27), calls=%async_computation.8 | async-start | bytes 262144
  66.2 2.4 copy-start.10
  69.6 3.6 %collective-permute-start.13 = (bf16[192,4096]{1,0:T(8,128)(2,1)S(1)}, bf16[192,4096]{1,0:T(8,128)(2,1)S(1)}, u32[]{:S(2)}, u32[]{:S(2)}) collective-permute-start(bf16[192,4096]{1,0:T(8,128)(2,1)S(1)} %convolution_convert_fusion.2), channel_id=1, source_target_pairs={{0,1},{1,0},{2,3},{3,2},{4,5},{5,4},{6,7},{7,6},{8,9},{9,8},{10,11... | collective-permute-start | bytes 4718600 | tf_op jit(solution)/shard_map/ppermute | solution.py:68
  73.2 41.4 %copy-start.2 = (bf16[24,4096]{1,0:T(8,128)(2,1)S(1)}, bf16[24,4096]{1,0:T(8,128)(2,1)}, u32[]{:S(2)}) copy-start(bf16[24,4096]{1,0:T(8,128)(2,1)} %param.9) | copy-start | bytes 589828
  75.5 80.0 %all-gather.6.cloned.1.call-start = ((), (), s32[]{:S(2)}) async-start(), calls=%async_computation.4 | async-start | bytes 1769472 | tf_op jit(solution)/shard_map/all_gather | solution.py:125
  116.3 102.7 %reduce-scatter.5.cloned.1.call-start = ((), (), s32[]{:S(2)}) async-start(), calls=%async_computation.5 | async-start | bytes 1769472 | tf_op jit(solution)/shard_map/reduce_scatter | solution.py:114
  118.1 43.5 %collective-permute-start.15 = (bf16[256,4096]{1,0:T(8,128)(2,1)S(1)}, bf16[256,4096]{1,0:T(8,128)(2,1)}, u32[]{:S(2)}, u32[]{:S(2)}) collective-permute-start(bf16[256,4096]{1,0:T(8,128)(2,1)S(1)} %constant_dynamic-slice_fusion), channel_id=1, source_target_pairs={{0,128},{128,0},{1,129},{129,1},{2,130},{130,2},{3,131},{131,3},{4... | collective-permute-start | bytes 6291464 | tf_op jit(solution)/shard_map/ppermute | solution.py:106
  155.5 6.1 %collective-permute-start.16 = (bf16[192,4096]{1,0:T(8,128)(2,1)}, bf16[192,4096]{1,0:T(8,128)(2,1)}, u32[]{:S(2)}, u32[]{:S(2)}) collective-permute-start(bf16[192,4096]{1,0:T(8,128)(2,1)} %all-gather.6.cloned.1.call-done), channel_id=1, source_target_pairs={{0,1},{1,0},{2,3},{3,2},{4,5},{5,4},{6,7},{7,6},{8,9},{9,8},{10,11... | collective-permute-start | bytes 4718600 | tf_op jit(solution)/shard_map/ppermute | solution.py:68
  155.5 6.1 %collective-permute-start.14 = (f32[2,256]{1,0:T(2,128)S(1)}, f32[2,256]{1,0:T(2,128)S(1)}, u32[]{:S(2)}, u32[]{:S(2)}) collective-permute-start(f32[2,256]{1,0:T(2,128)S(1)} %constant_dynamic-slice_fusion.1), channel_id=1, source_target_pairs={{0,128},{128,0},{1,129},{129,1},{2,130},{130,2},{3,131},{131,3},{4... | collective-permute-start | bytes 6152 | tf_op jit(solution)/shard_map/ppermute | solution.py:107
  168.1 50.9 %copy-start.3 = (bf16[24,4096]{1,0:T(8,128)(2,1)S(1)}, bf16[24,4096]{1,0:T(8,128)(2,1)}, u32[]{:S(2)}) copy-start(bf16[24,4096]{1,0:T(8,128)(2,1)} %reduce-scatter.3.cloned.1.call-done) | copy-start | bytes 589828
  168.1 3.8 %collective-permute-start.17 = (bf16[192,4096]{1,0:T(8,128)(2,1)}, bf16[192,4096]{1,0:T(8,128)(2,1)}, u32[]{:S(2)}, u32[]{:S(2)}) collective-permute-start(bf16[192,4096]{1,0:T(8,128)(2,1)} %convolution_convert_fusion), channel_id=1, source_target_pairs={{0,1},{1,0},{2,3},{3,2},{4,5},{5,4},{6,7},{7,6},{8,9},{9,8},{10,11... | collective-permute-start | bytes 4718600 | tf_op jit(solution)/shard_map/ppermute | solution.py:68
  178.8 81.1 %all-gather.8.cloned.1.call-start = ((), (), s32[]{:S(2)}) async-start(), calls=%async_computation.6 | async-start | bytes 1769472 | tf_op jit(solution)/shard_map/all_gather | solution.py:134
  259.9 4.3 %copy-start.12 = (f32[192,512]{1,0:T(8,128)S(1)}, f32[192,512]{1,0:T(8,128)}, u32[]{:S(2)}) copy-start(f32[192,512]{1,0:T(8,128)} %get-tuple-element.70) | copy-start | bytes 1179652
  259.9 4.2 %collective-permute-start.18 = (bf16[192,4096]{1,0:T(8,128)(2,1)}, bf16[192,4096]{1,0:T(8,128)(2,1)S(1)}, u32[]{:S(2)}, u32[]{:S(2)}) collective-permute-start(bf16[192,4096]{1,0:T(8,128)(2,1)} %all-gather.8.cloned.1.call-done), channel_id=1, source_target_pairs={{0,1},{1,0},{2,3},{3,2},{4,5},{5,4},{6,7},{7,6},{8,9},{9,8},{10,11... | collective-permute-start | bytes 4718600 | tf_op jit(solution)/shard_map/ppermute | solution.py:68
  264.1 4.5 %copy-start.11 = (bf16[192,4096]{1,0:T(8,128)(2,1)}, bf16[192,4096]{1,0:T(8,128)(2,1)S(1)}, u32[]{:S(2)}) copy-start(bf16[192,4096]{1,0:T(8,128)(2,1)S(1)} %collective-permute-done.18) | copy-start | bytes 4718596
  264.1 4.7 %copy-start.9 = (bf16[192,4096]{1,0:T(8,128)(2,1)S(1)}, bf16[192,4096]{1,0:T(8,128)(2,1)}, u32[]{:S(2)}) copy-start(bf16[192,4096]{1,0:T(8,128)(2,1)} %all-gather.4.cloned.1.call-done) | copy-start | bytes 4718596
  274.9 15.9 %collective-permute-start.21 = (bf16[64,4224]{1,0:T(8,128)(2,1)S(1)}, bf16[64,4224]{1,0:T(8,128)(2,1)S(1)}, u32[]{:S(2)}, u32[]{:S(2)}) collective-permute-start(bf16[64,4224]{1,0:T(8,128)(2,1)S(1)} %get-tuple-element.48), channel_id=1, source_target_pairs={{0,4},{4,8},{8,12},{12,0},{1,5},{5,9},{9,13},{13,1},{2,6},{6,10},{... | collective-permute-start | bytes 1622024 | tf_op jit(solution)/shard_map/ppermute | solution.py:42
  276.4 26.9 %collective-permute-start.20 = (bf16[64,4224]{1,0:T(8,128)(2,1)S(1)}, bf16[64,4224]{1,0:T(8,128)(2,1)S(1)}, u32[]{:S(2)}, u32[]{:S(2)}) collective-permute-start(bf16[64,4224]{1,0:T(8,128)(2,1)S(1)} %get-tuple-element.49), channel_id=1, source_target_pairs={{0,8},{4,12},{8,0},{12,4},{1,9},{5,13},{9,1},{13,5},{2,10},{6,14},... | collective-permute-start | bytes 1622024 | tf_op jit(solution)/shard_map/ppermute | solution.py:42
  279.2 24.2 %collective-permute-start.19 = (bf16[64,4224]{1,0:T(8,128)(2,1)S(1)}, bf16[64,4224]{1,0:T(8,128)(2,1)S(1)}, u32[]{:S(2)}, u32[]{:S(2)}) collective-permute-start(bf16[64,4224]{1,0:T(8,128)(2,1)S(1)} %get-tuple-element.44), channel_id=1, source_target_pairs={{0,12},{4,0},{8,4},{12,8},{1,13},{5,1},{9,5},{13,9},{2,14},{6,2},{... | collective-permute-start | bytes 1622024 | tf_op jit(solution)/shard_map/ppermute | solution.py:42
  280.6 22.8 %collective-permute-start.27 = (bf16[64,4224]{1,0:T(8,128)(2,1)S(1)}, bf16[64,4224]{1,0:T(8,128)(2,1)S(1)}, u32[]{:S(2)}, u32[]{:S(2)}) collective-permute-start(bf16[64,4224]{1,0:T(8,128)(2,1)S(1)} %get-tuple-element.45), channel_id=1, source_target_pairs={{0,128},{128,2},{2,130},{130,0},{1,129},{129,3},{3,131},{131,1},{4... | collective-permute-start | bytes 1622024 | tf_op jit(solution)/shard_map/ppermute | solution.py:49
  282.1 21.3 %collective-permute-start.26 = (bf16[64,4224]{1,0:T(8,128)(2,1)S(1)}, bf16[64,4224]{1,0:T(8,128)(2,1)S(1)}, u32[]{:S(2)}, u32[]{:S(2)}) collective-permute-start(bf16[64,4224]{1,0:T(8,128)(2,1)S(1)} %get-tuple-element.46), channel_id=1, source_target_pairs={{0,2},{128,130},{2,0},{130,128},{1,3},{129,131},{3,1},{131,129},{4... | collective-permute-start | bytes 1622024 | tf_op jit(solution)/shard_map/ppermute | solution.py:49
  290.8 33.3 %copy-start.6 = (f32[2,32]{1,0:T(2,128)S(1)}, f32[2,32]{1,0:T(2,128)}, u32[]{:S(2)}) copy-start(f32[2,32]{1,0:T(2,128)} %param.13) | copy-start | bytes 772
  290.8 33.3 %copy-start.7 = (f32[2,32]{1,0:T(2,128)S(1)}, f32[2,32]{1,0:T(2,128)}, u32[]{:S(2)}) copy-start(f32[2,32]{1,0:T(2,128)} %param.16) | copy-start | bytes 772
  290.8 33.3 %copy-start.8 = (f32[2,32]{1,0:T(2,128)S(1)}, f32[2,32]{1,0:T(2,128)}, u32[]{:S(2)}) copy-start(f32[2,32]{1,0:T(2,128)} %param.17) | copy-start | bytes 772
  290.8 33.9 %copy-start.1 = (f32[32,4096]{1,0:T(8,128)S(1)}, f32[32,4096]{1,0:T(8,128)}, u32[]{:S(2)}) copy-start(f32[32,4096]{1,0:T(8,128)} %param.12) | copy-start | bytes 1572868
  290.8 33.9 %copy-start.4 = (f32[32,4096]{1,0:T(8,128)S(1)}, f32[32,4096]{1,0:T(8,128)}, u32[]{:S(2)}) copy-start(f32[32,4096]{1,0:T(8,128)} %param.14) | copy-start | bytes 1572868
  290.8 33.9 %copy-start.5 = (f32[32,4096]{1,0:T(8,128)S(1)}, f32[32,4096]{1,0:T(8,128)}, u32[]{:S(2)}) copy-start(f32[32,4096]{1,0:T(8,128)} %param.15) | copy-start | bytes 1572868
  290.8 17.8 %collective-permute-start.25 = (bf16[64,4224]{1,0:T(8,128)(2,1)S(1)}, bf16[64,4224]{1,0:T(8,128)(2,1)S(1)}, u32[]{:S(2)}, u32[]{:S(2)}) collective-permute-start(bf16[64,4224]{1,0:T(8,128)(2,1)S(1)} %get-tuple-element.47), channel_id=1, source_target_pairs={{0,130},{128,0},{2,128},{130,2},{1,131},{129,1},{3,129},{131,3},{4... | collective-permute-start | bytes 1622024 | tf_op jit(solution)/shard_map/ppermute | solution.py:49
  309.3 9.7 %collective-permute-start.30 = (bf16[16,4224]{1,0:T(8,128)(2,1)S(1)}, bf16[16,4224]{1,0:T(8,128)(2,1)S(1)}, u32[]{:S(2)}, u32[]{:S(2)}) collective-permute-start(bf16[16,4224]{1,0:T(8,128)(2,1)S(1)} %get-tuple-element.56), channel_id=1, source_target_pairs={{0,4},{4,8},{8,12},{12,0},{1,5},{5,9},{9,13},{13,1},{2,6},{6,10},{... | collective-permute-start | bytes 405512 | tf_op jit(solution)/shard_map/ppermute | solution.py:42
  309.9 9.0 %collective-permute-start.29 = (bf16[16,4224]{1,0:T(8,128)(2,1)S(1)}, bf16[16,4224]{1,0:T(8,128)(2,1)S(1)}, u32[]{:S(2)}, u32[]{:S(2)}) collective-permute-start(bf16[16,4224]{1,0:T(8,128)(2,1)S(1)} %get-tuple-element.57), channel_id=1, source_target_pairs={{0,8},{4,12},{8,0},{12,4},{1,9},{5,13},{9,1},{13,5},{2,10},{6,14},... | collective-permute-start | bytes 405512 | tf_op jit(solution)/shard_map/ppermute | solution.py:42
  311.1 8.5 %collective-permute-start.28 = (bf16[16,4224]{1,0:T(8,128)(2,1)S(1)}, bf16[16,4224]{1,0:T(8,128)(2,1)S(1)}, u32[]{:S(2)}, u32[]{:S(2)}) collective-permute-start(bf16[16,4224]{1,0:T(8,128)(2,1)S(1)} %get-tuple-element.55), channel_id=1, source_target_pairs={{0,12},{4,0},{8,4},{12,8},{1,13},{5,1},{9,5},{13,9},{2,14},{6,2},{... | collective-permute-start | bytes 405512 | tf_op jit(solution)/shard_map/ppermute | solution.py:42
  312.7 6.9 %collective-permute-start.24 = (bf16[16,4224]{1,0:T(8,128)(2,1)S(1)}, bf16[16,4224]{1,0:T(8,128)(2,1)S(1)}, u32[]{:S(2)}, u32[]{:S(2)}) collective-permute-start(bf16[16,4224]{1,0:T(8,128)(2,1)S(1)} %get-tuple-element.53), channel_id=1, source_target_pairs={{0,128},{128,2},{2,130},{130,0},{1,129},{129,3},{3,131},{131,1},{4... | collective-permute-start | bytes 405512 | tf_op jit(solution)/shard_map/ppermute | solution.py:49
  313.4 7.4 %collective-permute-start.23 = (bf16[16,4224]{1,0:T(8,128)(2,1)S(1)}, bf16[16,4224]{1,0:T(8,128)(2,1)S(1)}, u32[]{:S(2)}, u32[]{:S(2)}) collective-permute-start(bf16[16,4224]{1,0:T(8,128)(2,1)S(1)} %get-tuple-element.54), channel_id=1, source_target_pairs={{0,2},{128,130},{2,0},{130,128},{1,3},{129,131},{3,1},{131,129},{4... | collective-permute-start | bytes 405512 | tf_op jit(solution)/shard_map/ppermute | solution.py:49
  318.9 5.0 %collective-permute-start.22 = (bf16[16,4224]{1,0:T(8,128)(2,1)S(1)}, bf16[16,4224]{1,0:T(8,128)(2,1)S(1)}, u32[]{:S(2)}, u32[]{:S(2)}) collective-permute-start(bf16[16,4224]{1,0:T(8,128)(2,1)S(1)} %get-tuple-element.52), channel_id=1, source_target_pairs={{0,130},{128,0},{2,128},{130,2},{1,131},{129,1},{3,129},{131,3},{4... | collective-permute-start | bytes 405512 | tf_op jit(solution)/shard_map/ppermute | solution.py:49
Sparse Core Ops, SparseCore 0:
  19.2 39.6 all-gather.3
  75.6 38.9 reduce-scatter.2
  116.9 38.5 all-gather.5
  178.9 40.0 reduce-scatter.4
  221.2 38.6 all-gather.7
